TPU v7x, 32 devices: a whole 2x2x4 slice. The times are simulated.
32 devices in a mesh: dp: 8 (over y, x, core), tensor: 4 (over z).
Axes of the slice: x: 2, y: 2, z: 4, core: 2. Of those that a mesh axis runs over, the one named last changes fastest.
Arguments:
- tokens: bfloat16 [32, 8192], P('tensor', 'dp'), may hold values from -6 to 6
- out_grad: bfloat16 [32, 8192], P('tensor', 'dp'), may hold values from -6 to 6
- gate_weight: bfloat16 [8192, 15360], P('dp', 'tensor'), may hold values from -0.0625 to 0.0625
- up_weight: bfloat16 [8192, 15360], P('dp', 'tensor'), may hold values from -0.0625 to 0.0625
- down_weight: bfloat16 [15360, 8192], P('tensor', 'dp'), may hold values from -0.046875 to 0.046875
- gate_mask: int32 [64, 120], P('dp', 'tensor'), may hold values from 0 to 1
- up_mask: int32 [64, 120], P('dp', 'tensor'), may hold values from 0 to 1
- down_mask: int32 [120, 64], P('tensor', 'dp'), may hold values from 0 to 1
- counts: int32 [4], P('tensor'), may hold values from 1 to 8, 24 in all
Outputs:
- d_tokens: bfloat16 [32, 8192], P('tensor', 'dp')
- gate_sum: float32 [8192, 15360], P('dp', 'tensor')
- up_sum: float32 [8192, 15360], P('dp', 'tensor')
- down_sum: float32 [15360, 8192], P('tensor', 'dp')
Inputs may be any that keep to these rules, and one draw needn't show every extreme that they name: counts[t] live rows open the t-th block of 8 token rows; at least one block is full.
All inputs are finite; a program needn't handle non-finite values.
Results may differ from a plain program's by a relative error of at most 0.005.
Values may be sent and summed in bfloat16 or wider, within the bound.
A program may use at most 128 MiB of HBM per device.

v0:
```python
import jax
import jax.numpy as jnp
from jax import lax
from jax.sharding import PartitionSpec as P


def expand(mask, side):
    return jnp.repeat(jnp.repeat(mask, side, axis=0), side, axis=1)


def contract_rows(left, right):
    return lax.dot_general(
        left, right, (((0,), (0,)), ((), ())), preferred_element_type=jnp.float32
    )


def contract_cols(left, right):
    return lax.dot_general(
        left, right, (((1,), (1,)), ((), ())), preferred_element_type=jnp.float32
    )


def swiglu_parts(gate_pre, up_pre, hidden_grad):
    sigmoid_gate = jax.nn.sigmoid(gate_pre)
    activated = gate_pre * sigmoid_gate
    hidden = (activated * up_pre).astype(jnp.bfloat16)
    gate_grad = (
        hidden_grad * up_pre * sigmoid_gate * (1.0 + gate_pre * (1.0 - sigmoid_gate))
    ).astype(jnp.bfloat16)
    up_grad = (hidden_grad * activated).astype(jnp.bfloat16)
    return (hidden, gate_grad, up_grad)


def on_device(
    tokens, out_grad, gate_weight, up_weight, down_weight, gate_mask, up_mask, down_mask, counts
):
    side = gate_weight.shape[0] // gate_mask.shape[0]
    tok_rows = tokens.shape[0]
    hidden_width = gate_weight.shape[1]
    position = lax.broadcasted_iota(jnp.int32, (tok_rows, 1), 0)
    masked_cot = jnp.where(position < counts[0], out_grad, jnp.zeros_like(out_grad))
    gate_keep = expand(gate_mask, side)
    up_keep = expand(up_mask, side)
    down_keep = expand(down_mask, side)
    masked_gate = gate_weight * gate_keep.astype(jnp.bfloat16)
    masked_up = up_weight * up_keep.astype(jnp.bfloat16)
    masked_down = down_weight * down_keep.astype(jnp.bfloat16)
    all_tokens, all_cot = (
        lax.all_gather(tokens, "tensor", axis=0, tiled=True),
        lax.all_gather(masked_cot, "tensor", axis=0, tiled=True),
    )
    token_block = all_tokens
    cot_block = all_cot
    gate_pre = jnp.dot(token_block, masked_gate, preferred_element_type=jnp.float32)
    up_pre = jnp.dot(token_block, masked_up, preferred_element_type=jnp.float32)
    hidden_grad = contract_cols(cot_block, masked_down)
    summed = lax.psum_scatter(
        jnp.concatenate([gate_pre, up_pre, hidden_grad], axis=1),
        "dp",
        scatter_dimension=0,
        tiled=True,
    )
    hidden, gate_grad, up_grad = swiglu_parts(
        summed[:, :hidden_width],
        summed[:, hidden_width : 2 * hidden_width],
        summed[:, 2 * hidden_width :],
    )
    packed = jnp.concatenate([gate_grad, up_grad, hidden], axis=1)
    shard_piece = lax.all_gather(packed, "dp", axis=0, tiled=True)
    gate_part = shard_piece[:, :hidden_width]
    up_part = shard_piece[:, hidden_width : 2 * hidden_width]
    hidden_part = shard_piece[:, 2 * hidden_width :]
    token_block = all_tokens
    cot_block = all_cot
    row_grad = contract_cols(gate_part, masked_gate) + contract_cols(up_part, masked_up)
    gate_sum = contract_rows(token_block, gate_part)
    up_sum = contract_rows(token_block, up_part)
    down_sum = contract_rows(hidden_part, cot_block)
    d_tokens = lax.psum_scatter(row_grad, "tensor", scatter_dimension=0, tiled=True)
    return (
        d_tokens.astype(jnp.bfloat16),
        gate_sum * gate_keep.astype(jnp.float32),
        up_sum * up_keep.astype(jnp.float32),
        down_sum * down_keep.astype(jnp.float32),
    )


def solution(mesh):
    in_specs = (
        P("tensor", "dp"),
        P("tensor", "dp"),
        P("dp", "tensor"),
        P("dp", "tensor"),
        P("tensor", "dp"),
        P("dp", "tensor"),
        P("dp", "tensor"),
        P("tensor", "dp"),
        P("tensor"),
    )
    out_specs = (P("tensor", "dp"), P("dp", "tensor"), P("dp", "tensor"), P("tensor", "dp"))
    return jax.shard_map(
        on_device, mesh=mesh, in_specs=in_specs, out_specs=out_specs, check_vma=False
    )
```

profile of v0, /device:TPU:0, one launch (start us, length us, event | category | flops | bytes accessed | tf_op | source)
XLA Modules:
  0.0 235.0 jit_solution(4178601530871482305)
XLA Ops:
  10.5 0.8 broadcast_select_fusion
  11.3 14.9 %all_gather.10 = bf16[32,1024]{1,0:T(8,128)(2,1)S(1)} all-gather(bf16[8,1024]{1,0:T(8,128)(2,1)S(1)} %broadcast_select_fusion), channel_id=1, replica_groups=mesh['dp'=8,'tensor'=4] {'tensor'}, dimensions={0}, use_global_device_ids=true | all-gather | bytes 81920 | tf_op jit(solution)/shard_map/all_gather | solution.py:50
  26.4 13.5 %all_gather.9 = bf16[32,1024]{1,0:T(8,128)(2,1)S(1)} all-gather(bf16[8,1024]{1,0:T(8,128)(2,1)} %param.9), channel_id=1, replica_groups=mesh['dp'=8,'tensor'=4] {'tensor'}, dimensions={0}, use_global_device_ids=true | all-gather | bytes 81920 | tf_op jit(solution)/shard_map/all_gather | solution.py:49
  40.0 10.6 %copy.30 = bf16[1024,3840]{0,1:T(8,128)(2,1)} copy(bf16[1024,3840]{1,0:T(8,128)(2,1)} %param.11) | data formatting | bytes 15728640 | tf_op args[2]
  50.6 10.6 %copy.32 = bf16[1024,3840]{0,1:T(8,128)(2,1)} copy(bf16[1024,3840]{1,0:T(8,128)(2,1)} %param.12) | data formatting | bytes 15728640 | tf_op args[3]
  61.2 3.8 %bitcast_multiply_fusion.6 = bf16[1024,3840]{0,1:T(8,128)(2,1)S(1)} fusion(bf16[1024,3840]{0,1:T(8,128)(2,1)} %copy.30, bf16[1024,30]{0,1:T(8,128)(2,1)S(1)} %bitcast.72), kind=kLoop, calls=%fused_computation.7 | loop fusion | flops 3932160 | bytes 15790080 | tf_op jit(solution)/shard_map/mul | solution.py:45
  65.0 3.4 %convolution_bitcast_fusion.1 = f32[32,3840]{1,0:T(8,128)} fusion(bf16[1024,3840]{0,1:T(8,128)(2,1)S(1)} %bitcast_multiply_fusion.6, bf16[32,1024]{1,0:T(8,128)(2,1)S(1)} %all_gather.9), kind=kOutput, calls=%fused_computation.9 | convolution fusion | flops 251658240 | bytes 8421376 | tf_op jit(solution)/shard_map/dot_general | solution.py:54
  68.3 3.8 %bitcast_multiply_fusion.5 = bf16[1024,3840]{0,1:T(8,128)(2,1)S(1)} fusion(bf16[1024,3840]{0,1:T(8,128)(2,1)} %copy.32, bf16[1024,30]{0,1:T(8,128)(2,1)S(1)} %bitcast.73), kind=kLoop, calls=%fused_computation.6 | loop fusion | flops 3932160 | bytes 15790080 | tf_op jit(solution)/shard_map/mul | solution.py:46
  72.1 2.4 %convolution_bitcast_fusion = f32[32,3840]{1,0:T(8,128)S(1)} fusion(bf16[1024,3840]{0,1:T(8,128)(2,1)S(1)} %bitcast_multiply_fusion.5, bf16[32,1024]{1,0:T(8,128)(2,1)S(1)} %all_gather.9), kind=kOutput, calls=%fused_computation.8 | convolution fusion | flops 251658240 | bytes 8421376 | tf_op jit(solution)/shard_map/dot_general | solution.py:55
  74.6 4.8 %broadcast_in_dim.48 = bf16[3840,8,128]{2,1,0:T(8,128)(2,1)S(1)} broadcast(bf16[3840,8]{1,0:T(8,128)(2,1)S(1)} %bitcast.67), dimensions={0,1} | broadcast | bytes 7925760 | tf_op jit(solution)/shard_map/broadcast_in_dim | solution.py:8
  79.5 4.7 %fusion = f32[32,3840]{1,0:T(8,128)S(1)} fusion(bf16[32,1024]{1,0:T(8,128)(2,1)S(1)} %all_gather.10, bf16[3840,1024]{1,0:T(8,128)(2,1)} %param.13, bf16[480,8,8,128]{3,2,1,0:T(8,128)(2,1)S(1)} %bitcast.65), kind=kOutput, calls=%fused_computation.4 | convolution fusion | flops 255590400 | bytes 16285696 | tf_op jit(solution)/shard_map/dot_general | solution.py:18
  84.2 1.2 pad_maximum_fusion
  87.3 57.9 %all-reduce.3.cloned.1.call-done = f32[32,11520]{1,0:T(8,128)} async-done(((f32[32,11520]{1,0:T(8,128)}), f32[32,11520]{1,0:T(8,128)}) %all-reduce.3.cloned.1.call-update) | async-done | bytes 1474576
  145.2 1.2 multiply_convert_fusion.2
  146.4 9.5 %all-gather = bf16[8,4,11520]{2,1,0:T(4,128)(2,1)S(1)} all-gather(bf16[1,4,11520]{2,1,0:T(4,128)(2,1)S(1)} %maximum_bitcast_fusion), channel_id=1, replica_groups=mesh['dp'=8,'tensor'=4] {'dp'}, dimensions={0}, use_global_device_ids=true | all-gather | bytes 829440 | tf_op jit(solution)/shard_map/all_gather | solution.py:69
  156.1 4.7 %fusion.6 = f32[32,1024]{1,0:T(8,128)S(1)} fusion(bf16[1024,3840]{0,1:T(8,128)(2,1)} %copy-done.1, bf16[32,11520]{1,0:T(8,128)(2,1)S(1)} %reshape.32), kind=kOutput, calls=%fused_computation.16 | convolution fusion | flops 251658240 | bytes 8241152 | tf_op jit(solution)/shard_map/dot_general | solution.py:18
  160.7 5.3 %convolution_add_fusion = f32[32,1024]{1,0:T(8,128)} fusion(f32[32,1024]{1,0:T(8,128)S(1)} %fusion.6, bf16[1024,3840]{0,1:T(8,128)(2,1)} %copy-done, bf16[32,11520]{1,0:T(8,128)(2,1)S(1)} %reshape.32), kind=kOutput, calls=%fused_computation.11 | convolution fusion | flops 251691008 | bytes 8372224 | tf_op jit(solution)/shard_map/dot_general | solution.py:18
  166.3 4.5 %broadcast_in_dim.54 = f32[3840,8,128]{2,1,0:T(8,128)S(1)} broadcast(f32[3840,8]{1,0:T(8,128)S(1)} %bitcast.66), dimensions={0,1} | broadcast | bytes 15851520 | tf_op jit(solution)/shard_map/broadcast_in_dim | solution.py:8
  170.8 9.1 %bitcast_multiply_fusion = f32[3840,1024]{1,0:T(8,128)} fusion(f32[480,8,8,128]{3,2,1,0:T(8,128)S(1)} %bitcast.64, bf16[32,1024]{1,0:T(8,128)(2,1)S(1)} %all_gather.10, bf16[32,11520]{1,0:T(8,128)(2,1)S(1)} %reshape.32), kind=kOutput, calls=%fused_computation | convolution fusion | flops 255590400 | bytes 31768576 | tf_op jit(solution)/shard_map/dot_general | solution.py:12
  179.8 8.0 %bitcast_multiply_fusion.2 = f32[1024,3840]{0,1:T(8,128)} fusion(bf16[32,1024]{1,0:T(8,128)(2,1)S(1)} %all_gather.9, f32[1024,30]{0,1:T(8,128)S(1)} %bitcast.68, bf16[32,11520]{1,0:T(8,128)(2,1)S(1)} %reshape.32), kind=kOutput, calls=%fused_computation.2 | convolution fusion | flops 255590400 | bytes 16171008 | tf_op jit(solution)/shard_map/dot_general | solution.py:12
  187.9 15.6 %copy.37 = f32[1024,3840]{1,0:T(8,128)} copy(f32[1024,3840]{0,1:T(8,128)} %bitcast_multiply_fusion.2) | data formatting | bytes 31457280
  203.5 7.7 %bitcast_multiply_fusion.1 = f32[1024,3840]{0,1:T(8,128)} fusion(bf16[32,1024]{1,0:T(8,128)(2,1)S(1)} %all_gather.9, f32[1024,30]{0,1:T(8,128)S(1)} %bitcast.69, bf16[32,11520]{1,0:T(8,128)(2,1)S(1)} %reshape.32), kind=kOutput, calls=%fused_computation.1 | convolution fusion | flops 255590400 | bytes 16171008 | tf_op jit(solution)/shard_map/dot_general | solution.py:12
  211.2 15.6 %copy.38 = f32[1024,3840]{1,0:T(8,128)} copy(f32[1024,3840]{0,1:T(8,128)} %bitcast_multiply_fusion.1) | data formatting | bytes 31457280
  226.8 1.4 convert_element_type.90
  (40 shorter events, 4.5 us)
Async XLA Ops:
  7.2 138.0 %all-reduce.3.cloned.1.call-start = ((), (), s32[]{:S(2)}) async-start(), calls=%async_computation.2 | async-start | bytes 2949120
  64.9 3.4 %copy-start.1 = (bf16[1024,3840]{0,1:T(8,128)(2,1)}, bf16[1024,3840]{0,1:T(8,128)(2,1)S(1)}, u32[]{:S(2)}) copy-start(bf16[1024,3840]{0,1:T(8,128)(2,1)S(1)} %bitcast_multiply_fusion.6) | copy-start | bytes 23592964
  72.1 7.3 %copy-start = (bf16[1024,3840]{0,1:T(8,128)(2,1)}, bf16[1024,3840]{0,1:T(8,128)(2,1)S(1)}, u32[]{:S(2)}) copy-start(bf16[1024,3840]{0,1:T(8,128)(2,1)S(1)} %bitcast_multiply_fusion.5) | copy-start | bytes 23592964
  79.4 4.7 %copy-start.2 = (f32[32,3840]{1,0:T(8,128)S(1)}, f32[32,3840]{1,0:T(8,128)}, u32[]{:S(2)}) copy-start(f32[32,3840]{1,0:T(8,128)} %convolution_bitcast_fusion.1) | copy-start | bytes 1474564
  79.4 6.6 %copy-start.3 = (u32[32]{0:T(128)S(1)}, u32[32]{0:T(128)}, u32[]{:S(2)}) copy-start(u32[32]{0:T(128)} %constant.10) | copy-start | bytes 388
  85.4 141.4 %reduce-scatter.2.cloned.1.call-start = ((), (), s32[]{:S(2)}) async-start(), calls=%async_computation.1 | async-start | bytes 163840 | tf_op jit(solution)/shard_map/reduce_scatter | solution.py:79
Sparse Core Ops, SparseCore 0:
  85.5 59.5 all-reduce.2
  166.2 19.1 reduce-scatter.1
where the time goes:
time: 236 us; the launch traced here: 235 us
  local copies, waits for them, and re-layouts  63.8 us (27%)
  waiting for transfers between devices  57.9 us (25%)
  matrix products  45.3 us (19%)
  blocking collectives  38 us (16%)
  between operations  15.6 us (7%)
  other arithmetic  14.4 us (6%)
    unnamed x3, waiting for transfers between devices  57.9 us
    unnamed x26, local copies, waits for them, and re-layouts  53.7 us
    dot_general x3, matrix products, contract_rows(): lax.dot_general(left, right, (((0,), (0,)), ((), ())), preferred_element_...  24.8 us
    all_gather x1, blocking collectives, on_device(): lax.all_gather(masked_cot, 'tensor', axis=0, tiled=True)  14.9 us
    dot_general x3, matrix products, contract_cols(): lax.dot_general(left, right, (((1,), (1,)), ((), ())), preferred_element_...  14.7 us
    all_gather x1, blocking collectives, on_device(): lax.all_gather(tokens, 'tensor', axis=0, tiled=True)  13.5 us
    broadcast_in_dim x4, local copies, waits for them, and re-layouts, expand(): return jnp.repeat(jnp.repeat(mask, side, axis=0), side, axis=1)  9.57 us
    all_gather x1, blocking collectives, on_device(): shard_piece = lax.all_gather(packed, 'dp', axis=0, tiled=True)  9.52 us
  transfers between devices with their start and end apart: 2, of which 1 were waited for; matrix products, arithmetic and copies ran while one was open for 26% of the time, Pallas kernels for 0%

commit v1 on v0

v1 whole, which is shorter than its diff:
```python
import functools

import jax
import jax.numpy as jnp
from jax import lax
from jax.experimental import pallas as pl
from jax.experimental.pallas import tpu as pltpu
from jax.sharding import PartitionSpec as P

MESH = pl.DeviceIdType.MESH
LANES = 128
bf16, f32 = jnp.bfloat16, jnp.float32


def dot_nn(a, b):
    return jnp.dot(a, b, preferred_element_type=f32)


def dot_nt(a, b):
    return lax.dot_general(a, b, (((1,), (1,)), ((), ())), preferred_element_type=f32)


def splat(value):
    return jnp.full((16, LANES), value.astype(f32), f32).astype(bf16)


def masked_tile(block, keeps):
    keep = jnp.concatenate([splat(k) for k in keeps], axis=1) if len(keeps) > 1 else splat(keeps[0])
    rows, cols = block.shape
    return (block.reshape(rows // 16, 16, cols) * keep[None]).reshape(rows, cols)


def swiglu_parts(gate_pre, up_pre, hidden_grad):
    sig = jax.nn.sigmoid(gate_pre)
    activated = gate_pre * sig
    hidden = (activated * up_pre).astype(bf16)
    gate_grad = (hidden_grad * up_pre * sig * (1.0 + gate_pre * (1.0 - sig))).astype(bf16)
    up_grad = (hidden_grad * activated).astype(bf16)
    return gate_grad, up_grad, hidden


def exchange_kernel(
    ndp, nt, nq, pw, nchunk,
    tok_ref, cot_ref, gate_hbm, up_hbm, down_hbm, gmask, umask, dmask, counts,
    dtok_ref, act_ref, tokall_ref, cotall_ref,
    gw, uw, dw, xs, snd1, own1, rcv1, snd2, rcv2, acts, dacc, dsnd, drcv,
    wsem, xs_s, xs_r, s1_s, s1_r, s2_s, s2_r, ag_s, ag_r, fw_s, fw_r, dt_s, dt_r,
):
    nchip = ndp // 2
    tr, width = tok_ref.shape
    kblocks = width // LANES
    me = lax.axis_index("dp")
    mt = lax.axis_index("tensor")
    core = lax.rem(me, 2)
    chip = me // 2
    sibling = chip * 2 + (1 - core)

    def weight_copies(q):
        cols = pl.ds(pl.multiple_of(q * pw, pw), pw)
        return (
            pltpu.make_async_copy(gate_hbm.at[:, cols], gw.at[q], wsem.at[q, 0]),
            pltpu.make_async_copy(up_hbm.at[:, cols], uw.at[q], wsem.at[q, 1]),
            pltpu.make_async_copy(down_hbm.at[cols, :], dw.at[q], wsem.at[q, 2]),
        )

    def each_piece(c, k, last):
        return c * ndp + 2 * k + (core if last else 1 - core)

    for c in range(nchunk):
        def load(k, _, c=c):
            for last in (False, True):
                q = each_piece(c, k, last)

                @pl.when(q < nq)
                def _():
                    for copy in weight_copies(q):
                        copy.start()
            return 0
        lax.fori_loop(0, nchip, load, 0)

    live = lax.broadcasted_iota(jnp.int32, (tr, width), 0) < counts[0]
    cot = jnp.where(live, cot_ref[...].astype(f32), 0.0)
    xs[mt] = jnp.concatenate([tok_ref[...].astype(f32), cot], axis=0).astype(bf16)

    barrier = pltpu.get_barrier_semaphore()
    pl.semaphore_signal(barrier, inc=1, device_id=(sibling, mt), device_id_type=MESH)

    def greet_chip(j, _):
        peer = lax.rem(chip + j, nchip) * 2 + core
        pl.semaphore_signal(barrier, inc=1, device_id=(peer, mt), device_id_type=MESH)
        return 0

    def greet_tensor(j, _):
        pl.semaphore_signal(barrier, inc=1, device_id=(me, lax.rem(mt + j, nt)), device_id_type=MESH)
        return 0

    lax.fori_loop(1, nchip, greet_chip, 0)
    lax.fori_loop(1, nt, greet_tensor, 0)
    pl.semaphore_wait(barrier, 1 + (nchip - 1) + (nt - 1))

    def x_copy(slot, j, peer):
        return pltpu.make_async_remote_copy(
            src_ref=xs.at[slot], dst_ref=xs.at[slot], send_sem=xs_s.at[j],
            recv_sem=xs_r.at[slot], device_id=(me, peer), device_id_type=MESH)

    def x_send(j, _):
        x_copy(mt, j, lax.rem(mt + j, nt)).start()
        return 0

    def x_wait(j, _):
        peer = lax.rem(mt + j, nt)
        x_copy(peer, j, peer).wait_recv()
        return 0

    def x_sent(j, _):
        x_copy(mt, j, lax.rem(mt + j, nt)).wait_send()
        return 0

    lax.fori_loop(1, nt, x_send, 0)
    lax.fori_loop(1, nt, x_wait, 0)
    gathered = xs[...].astype(f32)
    tokall_ref[...] = gathered[:, :tr].reshape(nt * tr, width).astype(bf16)
    cotall_ref[...] = gathered[:, tr:].reshape(nt * tr, width).astype(bf16)
    rows = nt * tr

    def forward_piece(q, out):
        @pl.when(q < nq)
        def _():
            for copy in weight_copies(q):
                copy.wait()
            per = pw // LANES
            for w, mask, slot in ((gw, gmask, 0), (uw, umask, 1)):
                for kb in range(kblocks):
                    span = pl.ds(kb * LANES, LANES)
                    w[q, span, :] = masked_tile(w[q, span, :], [mask[kb, q * per + i] for i in range(per)])
                out[slot] = dot_nn(tokall_ref[...], w[q])
            for i in range(per):
                span = pl.ds(i * LANES, LANES)
                dw[q, span, :] = masked_tile(dw[q, span, :], [dmask[q * per + i, kb] for kb in range(kblocks)])
            out[2] = dot_nt(cotall_ref[...], dw[q])

        @pl.when(q >= nq)
        def _():
            out[...] = jnp.zeros(out.shape, out.dtype)

    def copy1(c, k):
        return pltpu.make_async_remote_copy(
            src_ref=snd1.at[c, k], dst_ref=rcv1.at[c, k], send_sem=s1_s.at[c, k],
            recv_sem=s1_r.at[c, k], device_id=(sibling, mt), device_id_type=MESH)

    def forward(c):
        def step(k, _):
            forward_piece(each_piece(c, k, False), snd1.at[c, k])
            copy1(c, k).start()
            forward_piece(each_piece(c, k, True), own1.at[c, k])
            return 0
        lax.fori_loop(0, nchip, step, 0)

    def copy2(c, slot, k):
        return pltpu.make_async_remote_copy(
            src_ref=snd2.at[c, k], dst_ref=rcv2.at[c, slot], send_sem=s2_s.at[c, k],
            recv_sem=s2_r.at[c, slot], device_id=(k * 2 + core, mt), device_id_type=MESH)

    def reduce_send(c):
        def step(j, _):
            k = lax.rem(chip + j, nchip)
            copy1(c, k).wait_recv()
            snd2[c, k] = (own1[c, k] + rcv1[c, k]).astype(bf16)
            copy2(c, chip, k).start()
            return 0
        lax.fori_loop(1, nchip, step, 0)
        copy1(c, chip).wait_recv()

    def gather_copy(c, origin, sem, k):
        slot = c * ndp + origin
        return pltpu.make_async_remote_copy(
            src_ref=acts.at[slot], dst_ref=acts.at[slot], send_sem=ag_s.at[c, sem],
            recv_sem=ag_r.at[c, origin // 2], device_id=(k * 2 + core, mt), device_id_type=MESH)

    def sibling_copy(c, origin):
        slot = c * ndp + origin
        return pltpu.make_async_remote_copy(
            src_ref=acts.at[slot], dst_ref=acts.at[slot], send_sem=fw_s.at[c, origin // 2],
            recv_sem=fw_r.at[c, origin // 2], device_id=(sibling, mt), device_id_type=MESH)

    def activate(c):
        own1[c, chip] = own1[c, chip] + rcv1[c, chip]

        def add(j, _):
            k = lax.rem(chip + j, nchip)
            copy2(c, k, k).wait_recv()
            own1[c, chip] = own1[c, chip] + rcv2[c, k].astype(f32)
            return 0
        lax.fori_loop(1, nchip, add, 0)
        parts = swiglu_parts(own1[c, chip, 0], own1[c, chip, 1], own1[c, chip, 2])
        for i in range(3):
            acts[c * ndp + me, i] = parts[i]

        def send(j, _):
            gather_copy(c, me, j, lax.rem(chip + j, nchip)).start()
            return 0
        lax.fori_loop(1, nchip, send, 0)
        sibling_copy(c, me).start()

    def forward_on(c):
        def step(j, _):
            k = lax.rem(chip + j, nchip)
            gather_copy(c, k * 2 + core, j, k).wait_recv()
            sibling_copy(c, k * 2 + core).start()
            return 0
        lax.fori_loop(1, nchip, step, 0)

        def wait(k, _):
            sibling_copy(c, k * 2 + 1 - core).wait_recv()
            return 0
        lax.fori_loop(0, nchip, wait, 0)

    def token_grad(lo, hi):
        def step(q, _):
            dacc[...] += dot_nt(acts[q, 0], gw[q]) + dot_nt(acts[q, 1], uw[q])
            return 0
        if hi > lo:
            lax.fori_loop(lo, hi, step, 0)

    dacc[...] = jnp.zeros(dacc.shape, f32)
    for c in range(nchunk):
        forward(c)
        if c > 0:
            activate(c - 1)
        reduce_send(c)
        if c > 0:
            forward_on(c - 1)
    done = min((nchunk - 1) * ndp, nq)
    token_grad(0, done // 2)
    activate(nchunk - 1)
    token_grad(done // 2, done)
    forward_on(nchunk - 1)
    token_grad(done, nq)

    dsnd[...] = dacc[...].reshape(nt, tr, width)

    def d_copy(slot, k):
        return pltpu.make_async_remote_copy(
            src_ref=dsnd.at[k], dst_ref=drcv.at[slot], send_sem=dt_s.at[k],
            recv_sem=dt_r.at[slot], device_id=(me, k), device_id_type=MESH)

    def d_send(j, _):
        k = lax.rem(mt + nt - j, nt)
        d_copy(mt, k).start()
        return 0

    lax.fori_loop(1, nt, d_send, 0)
    act_ref[...] = acts[...]
    lax.fori_loop(1, nt, x_sent, 0)
    for c in range(nchunk):
        def drain(k, _, c=c):
            copy1(c, k).wait_send()
            sibling_copy(c, k * 2 + core).wait_send()
            return 0

        def drain_chips(j, _, c=c):
            k = lax.rem(chip + j, nchip)
            copy2(c, chip, k).wait_send()
            gather_copy(c, me, j, k).wait_send()
            return 0
        lax.fori_loop(0, nchip, drain, 0)
        lax.fori_loop(1, nchip, drain_chips, 0)

    def d_add(j, total):
        k = lax.rem(mt + j, nt)
        d_copy(k, k).wait_recv()
        return total + drcv[k]

    dtok_ref[...] = lax.fori_loop(1, nt, d_add, dsnd[mt]).astype(bf16)

    def d_sent(j, _):
        d_copy(mt, lax.rem(mt + j, nt)).wait_send()
        return 0
    lax.fori_loop(1, nt, d_sent, 0)


def outer_kernel(
    pw, gmask, umask, dmask, tok_ref, cot_ref, act_ref, gsum_ref, usum_ref, dsum_ref, tok_t
):
    q = pl.program_id(0)
    width = tok_ref.shape[1]
    per = pw // LANES

    @pl.when(q == 0)
    def _():
        tok_t[...] = tok_ref[...].astype(f32).T.astype(bf16)

    for slot, mask, out in ((0, gmask, gsum_ref), (1, umask, usum_ref)):
        for kb in range(width // LANES):
            span = pl.ds(kb * LANES, LANES)
            block = dot_nn(tok_t[span, :], act_ref[0, slot])
            for i in range(per):
                cols = slice(i * LANES, (i + 1) * LANES)
                out[span, cols] = block[:, cols] * mask[kb, q * per + i].astype(f32)
    hidden_t = act_ref[0, 2].astype(f32).T.astype(bf16)
    for i in range(per):
        block = dot_nn(hidden_t[i * LANES:(i + 1) * LANES], cot_ref[...])
        for kb in range(width // LANES):
            cols = slice(kb * LANES, (kb + 1) * LANES)
            dsum_ref[pl.ds(i * LANES, LANES), cols] = block[:, cols] * dmask[q * per + i, kb].astype(f32)


def on_device(
    ndp, nt, tokens, out_grad, gate_weight, up_weight, down_weight, gate_mask, up_mask, down_mask, counts
):
    tr, width = tokens.shape
    hidden_width = gate_weight.shape[1]
    rows = nt * tr
    pw = 2 * LANES if hidden_width % (2 * LANES) == 0 else LANES
    nq = hidden_width // pw
    nchunk = -(-nq // ndp)
    nchip = ndp // 2
    vmem = pl.BlockSpec(memory_space=pltpu.VMEM)
    smem = pl.BlockSpec(memory_space=pltpu.SMEM)
    hbm = pl.BlockSpec(memory_space=pl.ANY)
    dma = pltpu.SemaphoreType.DMA
    piece = (3, rows, pw)
    d_tokens, act, tok_all, cot_all = pl.pallas_call(
        functools.partial(exchange_kernel, ndp, nt, nq, pw, nchunk),
        out_shape=(
            jax.ShapeDtypeStruct((tr, width), bf16),
            jax.ShapeDtypeStruct((nchunk * ndp,) + piece, bf16),
            jax.ShapeDtypeStruct((rows, width), bf16),
            jax.ShapeDtypeStruct((rows, width), bf16),
        ),
        in_specs=[vmem, vmem, hbm, hbm, hbm, smem, smem, smem, smem],
        out_specs=(vmem, vmem, vmem, vmem),
        scratch_shapes=[
            pltpu.VMEM((nq, width, pw), bf16),
            pltpu.VMEM((nq, width, pw), bf16),
            pltpu.VMEM((nq, pw, width), bf16),
            pltpu.VMEM((nt, 2 * tr, width), bf16),
            pltpu.VMEM((nchunk, nchip) + piece, f32),
            pltpu.VMEM((nchunk, nchip) + piece, f32),
            pltpu.VMEM((nchunk, nchip) + piece, f32),
            pltpu.VMEM((nchunk, nchip) + piece, bf16),
            pltpu.VMEM((nchunk, nchip) + piece, bf16),
            pltpu.VMEM((nchunk * ndp,) + piece, bf16),
            pltpu.VMEM((rows, width), f32),
            pltpu.VMEM((nt, tr, width), f32),
            pltpu.VMEM((nt, tr, width), f32),
            dma((nq, 3)),
            dma((nt,)), dma((nt,)),
            dma((nchunk, nchip)), dma((nchunk, nchip)),
            dma((nchunk, nchip)), dma((nchunk, nchip)),
            dma((nchunk, nchip)), dma((nchunk, nchip)),
            dma((nchunk, nchip)), dma((nchunk, nchip)),
            dma((nt,)), dma((nt,)),
        ],
        compiler_params=pltpu.CompilerParams(
            collective_id=0, has_side_effects=True, vmem_limit_bytes=58 * 2**20
        ),
        name="exchange",
    )(tokens, out_grad, gate_weight, up_weight, down_weight, gate_mask, up_mask, down_mask, counts)

    whole = lambda q, *_: (0, 0)
    gate_sum, up_sum, down_sum = pl.pallas_call(
        functools.partial(outer_kernel, pw),
        grid_spec=pltpu.PrefetchScalarGridSpec(
            num_scalar_prefetch=3,
            grid=(nq,),
            in_specs=[
                pl.BlockSpec((rows, width), whole),
                pl.BlockSpec((rows, width), whole),
                pl.BlockSpec((1,) + piece, lambda q, *_: (q, 0, 0, 0)),
            ],
            out_specs=[
                pl.BlockSpec((width, pw), lambda q, *_: (0, q)),
                pl.BlockSpec((width, pw), lambda q, *_: (0, q)),
                pl.BlockSpec((pw, width), lambda q, *_: (q, 0)),
            ],
            scratch_shapes=[pltpu.VMEM((width, rows), bf16)],
        ),
        out_shape=(
            jax.ShapeDtypeStruct((width, hidden_width), f32),
            jax.ShapeDtypeStruct((width, hidden_width), f32),
            jax.ShapeDtypeStruct((hidden_width, width), f32),
        ),
        compiler_params=pltpu.CompilerParams(vmem_limit_bytes=40 * 2**20),
        name="outer",
    )(gate_mask, up_mask, down_mask, tok_all, cot_all, act)
    return d_tokens, gate_sum, up_sum, down_sum


def solution(mesh):
    in_specs = (
        P("tensor", "dp"),
        P("tensor", "dp"),
        P("dp", "tensor"),
        P("dp", "tensor"),
        P("tensor", "dp"),
        P("dp", "tensor"),
        P("dp", "tensor"),
        P("tensor", "dp"),
        P("tensor"),
    )
    out_specs = (P("tensor", "dp"), P("dp", "tensor"), P("dp", "tensor"), P("tensor", "dp"))
    body = functools.partial(on_device, mesh.shape["dp"], mesh.shape["tensor"])
    return jax.shard_map(body, mesh=mesh, in_specs=in_specs, out_specs=out_specs, check_vma=False)
```

time: 236 us -> 66.4 us (0.28)
  Pallas kernels: 0 us -> 59.1 us
  local copies, waits for them, and re-layouts: 63.8 us -> 5.52 us
  waiting for transfers between devices: 57.9 us -> 0 us
  matrix products: 45.3 us -> 0 us
  blocking collectives: 38 us -> 0 us
  other arithmetic: 14.4 us -> 0 us
  between operations: 15.6 us -> 1.35 us
    pallas_call x0 -> x2, Pallas kernels: none -> 59.1 us  [the longest x1 41.7 us: on_device(): pl.pallas_call(functools.partial(exchange_kernel, ndp, nt, nq, pw, nchunk...]
    unnamed x3 -> x0, waiting for transfers between devices: 57.9 us -> none
    unnamed x26 -> x14, local copies, waits for them, and re-layouts: 53.7 us -> 5.52 us
    dot_general x8 -> x0, matrix products: 45.3 us -> none  [the longest x3 24.8 us: contract_rows(): lax.dot_general(left, right, (((0,), (0,)), ((), ())), preferred_element_...]
    all_gather x3 -> x0, blocking collectives: 38 us -> none  [the longest x1 14.9 us: on_device(): lax.all_gather(masked_cot, 'tensor', axis=0, tiled=True)]
    broadcast_in_dim x4 -> x0, local copies, waits for them, and re-layouts: 9.57 us -> none  [expand(): return jnp.repeat(jnp.repeat(mask, side, axis=0), side, axis=1)]
    mul x2 -> x0, other arithmetic: 7.52 us -> none  [the longest x1 3.76 us: on_device(): masked_up = up_weight * up_keep.astype(jnp.bfloat16)]
    convert_element_type x5 -> x0, other arithmetic: 4.82 us -> none  [the longest x1 1.37 us: on_device(): d_tokens.astype(jnp.bfloat16)]
  transfers between devices with their start and end apart: 2 -> 0, of which waited for: 1 -> 0; matrix products, arithmetic and copies ran while one was open for 26% -> 0% of each run, Pallas kernels for 0% -> 0%
where the time goes in v1:
time: 66.4 us; the launch traced here: 66 us
  Pallas kernels  59.1 us (89%)
  local copies, waits for them, and re-layouts  5.52 us (8%)
  between operations  1.35 us (2%)
    pallas_call x1, Pallas kernels, on_device(): pl.pallas_call(functools.partial(exchange_kernel, ndp, nt, nq, pw, nchunk...  41.7 us
    pallas_call x1, Pallas kernels, on_device(): pl.pallas_call(functools.partial(outer_kernel, pw), grid_spec=pltpu.Prefe...  17.4 us
    unnamed x14, local copies, waits for them, and re-layouts  5.52 us

profile of v1, /device:TPU:0, one launch (start us, length us, event | category | flops | bytes accessed | tf_op | source)
XLA Modules:
  0.0 66.0 jit_solution(1877425698508692883)
XLA Ops:
  0.6 0.0 copy-start.5
  0.6 0.0 copy-start.4
  1.3 1.4 %copy.13.dmask = s32[30,8]{1,0:T(8,128)} copy(s32[30,8]{0,1:T(8,128)} %param.16) | data formatting | bytes 1920 | tf_op args[7]
  2.7 0.0 copy-start.1
  2.7 41.7 %exchange.1 = (bf16[8,1024]{1,0:T(8,128)(2,1)}, bf16[16,3,32,256]{3,2,1,0:T(8,128)(2,1)}, bf16[32,1024]{1,0:T(8,128)(2,1)}, bf16[32,1024]{1,0:T(8,128)(2,1)}) custom-call(bf16[8,1024]{1,0:T(8,128)(2,1)} %tok_ref.1, bf16[8,1024]{1,0:T(8,128)(2,1)} %cot_ref.1, bf16[1024,3840]{1,0:T(8,128)(2,1)} %gate_hbm.1, bf16[1024,3840]{1,0:T(8,128)(2,1)} %up_hbm.1, ...), custom_call_target="tpu_custom_call" | custom-call | tf_op jit(solution)/shard_map/exchange/pallas_call | solution.py:323
  44.4 0.0 copy-done.5
  44.4 0.0 copy-done.4
  44.5 0.0 copy-done.1
  44.5 0.0 copy-start
  44.5 1.1 %copy-done = bf16[16,3,32,256]{3,2,1,0:T(8,128)(2,1)S(1)} copy-done((bf16[16,3,32,256]{3,2,1,0:T(8,128)(2,1)S(1)}, bf16[16,3,32,256]{3,2,1,0:T(8,128)(2,1)}, u32[]{:S(2)}) %copy-start) | copy-done | bytes 786456
  45.6 0.0 copy-start.2
  45.6 0.8 %copy-done.2 = bf16[32,1024]{1,0:T(8,128)(2,1)S(1)} copy-done((bf16[32,1024]{1,0:T(8,128)(2,1)S(1)}, bf16[32,1024]{1,0:T(8,128)(2,1)}, u32[]{:S(2)}) %copy-start.2) | copy-done | bytes 65560
  46.4 0.0 copy-start.3
  46.4 0.8 %copy-done.3 = bf16[32,1024]{1,0:T(8,128)(2,1)S(1)} copy-done((bf16[32,1024]{1,0:T(8,128)(2,1)S(1)}, bf16[32,1024]{1,0:T(8,128)(2,1)}, u32[]{:S(2)}) %copy-start.3) | copy-done | bytes 65560
  47.3 17.4 %outer.1 = (f32[1024,3840]{1,0:T(8,128)}, f32[1024,3840]{1,0:T(8,128)}, f32[3840,1024]{1,0:T(8,128)}) custom-call(s32[8,30]{1,0:T(8,128)S(1)} %copy-done.4, s32[8,30]{1,0:T(8,128)S(1)} %copy-done.5, s32[30,8]{1,0:T(8,128)S(1)} %copy-done.1, bf16[32,1024]{1,0:T(8,128)(2,1)S(1)} %copy-done.2, bf16[32,1024]{1,0:T(8,128)(2,1)S(1)} %copy-done.3, ...), custom_call_target="tpu_custom_call" | custom-call | tf_op jit(solution)/shard_map/outer/pallas_call | solution.py:362
  64.6 1.3 %copy.17 = bf16[8,1024]{1,0:T(8,128)(2,1)} copy(bf16[8,1024]{1,0:T(8,128)(2,1)} %get-tuple-element.22) | data formatting | bytes 32768
Async XLA Ops:
  0.6 43.8 %copy-start.5 = (s32[8,30]{1,0:T(8,128)S(1)}, s32[8,30]{1,0:T(8,128)}, u32[]{:S(2)}) copy-start(s32[8,30]{1,0:T(8,128)} %umask.3) | copy-start | bytes 2884
  0.6 43.8 %copy-start.4 = (s32[8,30]{1,0:T(8,128)S(1)}, s32[8,30]{1,0:T(8,128)}, u32[]{:S(2)}) copy-start(s32[8,30]{1,0:T(8,128)} %gmask.3) | copy-start | bytes 2884
  2.7 41.8 %copy-start.1 = (s32[30,8]{1,0:T(8,128)S(1)}, s32[30,8]{1,0:T(8,128)}, u32[]{:S(2)}) copy-start(s32[30,8]{1,0:T(8,128)} %copy.13.dmask) | copy-start | bytes 2884
  44.5 1.1 %copy-start = (bf16[16,3,32,256]{3,2,1,0:T(8,128)(2,1)S(1)}, bf16[16,3,32,256]{3,2,1,0:T(8,128)(2,1)}, u32[]{:S(2)}) copy-start(bf16[16,3,32,256]{3,2,1,0:T(8,128)(2,1)} %get-tuple-element.14.act_ref) | copy-start | bytes 2359300
  45.6 0.8 %copy-start.2 = (bf16[32,1024]{1,0:T(8,128)(2,1)S(1)}, bf16[32,1024]{1,0:T(8,128)(2,1)}, u32[]{:S(2)}) copy-start(bf16[32,1024]{1,0:T(8,128)(2,1)} %get-tuple-element.12.tok_ref) | copy-start | bytes 196612
  46.4 0.8 %copy-start.3 = (bf16[32,1024]{1,0:T(8,128)(2,1)S(1)}, bf16[32,1024]{1,0:T(8,128)(2,1)}, u32[]{:S(2)}) copy-start(bf16[32,1024]{1,0:T(8,128)(2,1)} %get-tuple-element.13.cot_ref) | copy-start | bytes 196612

commit v2 on v1

--- a/solution.py
+++ b/solution.py
@@ -20,14 +20,19 @@
     return lax.dot_general(a, b, (((1,), (1,)), ((), ())), preferred_element_type=f32)
 
 
-def splat(value):
-    return jnp.full((16, LANES), value.astype(f32), f32).astype(bf16)
-
-
-def masked_tile(block, keeps):
-    keep = jnp.concatenate([splat(k) for k in keeps], axis=1) if len(keeps) > 1 else splat(keeps[0])
-    rows, cols = block.shape
-    return (block.reshape(rows // 16, 16, cols) * keep[None]).reshape(rows, cols)
+def keep_tile(keeps):
+    tiles = [jnp.full((16, LANES), k.astype(f32), f32).astype(bf16) for k in keeps]
+    return jnp.concatenate(tiles, axis=1) if len(tiles) > 1 else tiles[0]
+
+
+def masked(rows, keeps):
+    count, cols = rows.shape
+    return (rows.reshape(count // 16, 16, cols) * keep_tile(keeps)[None]).reshape(count, cols)
+
+
+def masked_stack(rows, keep_lists):
+    copies = [masked(rows, keeps) for keeps in keep_lists]
+    return jnp.concatenate(copies, axis=0) if len(copies) > 1 else copies[0]
 
 
 def swiglu_parts(gate_pre, up_pre, hidden_grad):
@@ -42,9 +47,9 @@
 def exchange_kernel(
     ndp, nt, nq, pw, nchunk,
     tok_ref, cot_ref, gate_hbm, up_hbm, down_hbm, gmask, umask, dmask, counts,
-    dtok_ref, act_ref, tokall_ref, cotall_ref,
-    gw, uw, dw, xs, snd1, own1, rcv1, snd2, rcv2, acts, dacc, dsnd, drcv,
-    wsem, xs_s, xs_r, s1_s, s1_r, s2_s, s2_r, ag_s, ag_r, fw_s, fw_r, dt_s, dt_r,
+    dtok_ref, act_ref, x_ref,
+    gw, uw, dw, xs, tokall, cotall, snd1, own1, rcv1, snd2, rcv2, acts, dacc, dsnd, drcv,
+    wsem, out_sem, xs_s, xs_r, s1_s, s1_r, s2_s, s2_r, ag_s, ag_r, fw_s, fw_r, dt_s, dt_r,
 ):
     nchip = ndp // 2
     tr, width = tok_ref.shape
@@ -119,25 +124,28 @@
     lax.fori_loop(1, nt, x_send, 0)
     lax.fori_loop(1, nt, x_wait, 0)
     gathered = xs[...].astype(f32)
-    tokall_ref[...] = gathered[:, :tr].reshape(nt * tr, width).astype(bf16)
-    cotall_ref[...] = gathered[:, tr:].reshape(nt * tr, width).astype(bf16)
+    tokall[...] = gathered[:, :tr].reshape(nt * tr, width).astype(bf16)
+    cotall[...] = gathered[:, tr:].reshape(nt * tr, width).astype(bf16)
+    x_out = pltpu.make_async_copy(xs, x_ref, out_sem.at[nchunk])
+    x_out.start()
     rows = nt * tr
+    per = pw // LANES
+    pair = 2 if kblocks % 2 == 0 else 1
 
     def forward_piece(q, out):
         @pl.when(q < nq)
         def _():
             for copy in weight_copies(q):
                 copy.wait()
-            per = pw // LANES
-            for w, mask, slot in ((gw, gmask, 0), (uw, umask, 1)):
-                for kb in range(kblocks):
-                    span = pl.ds(kb * LANES, LANES)
-                    w[q, span, :] = masked_tile(w[q, span, :], [mask[kb, q * per + i] for i in range(per)])
-                out[slot] = dot_nn(tokall_ref[...], w[q])
-            for i in range(per):
-                span = pl.ds(i * LANES, LANES)
-                dw[q, span, :] = masked_tile(dw[q, span, :], [dmask[q * per + i, kb] for kb in range(kblocks)])
-            out[2] = dot_nt(cotall_ref[...], dw[q])
+            for w, mask, slot in ((gw, gmask, 0), (uw, umask, 1), (dw, dmask, 2)):
+                source = cotall if slot == 2 else tokall
+                left = masked_stack(
+                    source[...],
+                    [[mask[kb, q * per + i] for kb in range(kblocks)] for i in range(per)])
+                sums = dot_nt(left, w[q]) if slot == 2 else dot_nn(left, w[q])
+                for i in range(per):
+                    cols = slice(i * LANES, (i + 1) * LANES)
+                    out[slot, :, cols] = sums[i * rows:(i + 1) * rows, cols]
 
         @pl.when(q >= nq)
         def _():
@@ -217,10 +225,25 @@
 
     def token_grad(lo, hi):
         def step(q, _):
-            dacc[...] += dot_nt(acts[q, 0], gw[q]) + dot_nt(acts[q, 1], uw[q])
+            for first in range(0, kblocks, pair):
+                blocks = range(first, first + pair)
+                span = pl.ds(first * LANES, pair * LANES)
+                sums = None
+                for w, mask, slot in ((gw, gmask, 0), (uw, umask, 1)):
+                    left = masked_stack(
+                        acts[q, slot], [[mask[kb, q * per + i] for i in range(per)] for kb in blocks])
+                    term = dot_nt(left, w[q, span, :])
+                    sums = term if sums is None else sums + term
+                for i, kb in enumerate(blocks):
+                    cols = slice(i * LANES, (i + 1) * LANES)
+                    dacc[:, kb * LANES:(kb + 1) * LANES] += sums[i * rows:(i + 1) * rows, cols]
             return 0
         if hi > lo:
             lax.fori_loop(lo, hi, step, 0)
+
+    def act_out(c):
+        span = pl.ds(c * ndp, ndp)
+        return pltpu.make_async_copy(acts.at[span], act_ref.at[span], out_sem.at[c])
 
     dacc[...] = jnp.zeros(dacc.shape, f32)
     for c in range(nchunk):
@@ -230,11 +253,13 @@
         reduce_send(c)
         if c > 0:
             forward_on(c - 1)
+            act_out(c - 1).start()
     done = min((nchunk - 1) * ndp, nq)
     token_grad(0, done // 2)
     activate(nchunk - 1)
     token_grad(done // 2, done)
     forward_on(nchunk - 1)
+    act_out(nchunk - 1).start()
     token_grad(done, nq)
 
     dsnd[...] = dacc[...].reshape(nt, tr, width)
@@ -250,7 +275,6 @@
         return 0
 
     lax.fori_loop(1, nt, d_send, 0)
-    act_ref[...] = acts[...]
     lax.fori_loop(1, nt, x_sent, 0)
     for c in range(nchunk):
         def drain(k, _, c=c):
@@ -277,18 +301,25 @@
         d_copy(mt, lax.rem(mt + j, nt)).wait_send()
         return 0
     lax.fori_loop(1, nt, d_sent, 0)
+    x_out.wait()
+    for c in range(nchunk):
+        act_out(c).wait()
 
 
 def outer_kernel(
-    pw, gmask, umask, dmask, tok_ref, cot_ref, act_ref, gsum_ref, usum_ref, dsum_ref, tok_t
+    pw, gmask, umask, dmask, x_ref, act_ref, dtok_ref, dtok_out, gsum_ref, usum_ref, dsum_ref, tok_t, cot
 ):
     q = pl.program_id(0)
-    width = tok_ref.shape[1]
+    nt, pair_rows, width = x_ref.shape
+    tr = pair_rows // 2
     per = pw // LANES
 
     @pl.when(q == 0)
     def _():
-        tok_t[...] = tok_ref[...].astype(f32).T.astype(bf16)
+        gathered = x_ref[...].astype(f32)
+        tok_t[...] = gathered[:, :tr].reshape(nt * tr, width).T.astype(bf16)
+        cot[...] = gathered[:, tr:].reshape(nt * tr, width).astype(bf16)
+        dtok_out[...] = dtok_ref[...]
 
     for slot, mask, out in ((0, gmask, gsum_ref), (1, umask, usum_ref)):
         for kb in range(width // LANES):
@@ -299,10 +330,10 @@
                 out[span, cols] = block[:, cols] * mask[kb, q * per + i].astype(f32)
     hidden_t = act_ref[0, 2].astype(f32).T.astype(bf16)
     for i in range(per):
-        block = dot_nn(hidden_t[i * LANES:(i + 1) * LANES], cot_ref[...])
+        block = dot_nn(hidden_t[i * LANES:(i + 1) * LANES], cot[...])
         for kb in range(width // LANES):
             cols = slice(kb * LANES, (kb + 1) * LANES)
-            dsum_ref[pl.ds(i * LANES, LANES), cols] = block[:, cols] * dmask[q * per + i, kb].astype(f32)
+            dsum_ref[pl.ds(i * LANES, LANES), cols] = block[:, cols] * dmask[kb, q * per + i].astype(f32)
 
 
 def on_device(
@@ -320,21 +351,23 @@
     hbm = pl.BlockSpec(memory_space=pl.ANY)
     dma = pltpu.SemaphoreType.DMA
     piece = (3, rows, pw)
-    d_tokens, act, tok_all, cot_all = pl.pallas_call(
+    down_mask = down_mask.T
+    d_tokens, act, gathered = pl.pallas_call(
         functools.partial(exchange_kernel, ndp, nt, nq, pw, nchunk),
         out_shape=(
             jax.ShapeDtypeStruct((tr, width), bf16),
             jax.ShapeDtypeStruct((nchunk * ndp,) + piece, bf16),
-            jax.ShapeDtypeStruct((rows, width), bf16),
-            jax.ShapeDtypeStruct((rows, width), bf16),
+            jax.ShapeDtypeStruct((nt, 2 * tr, width), bf16),
         ),
         in_specs=[vmem, vmem, hbm, hbm, hbm, smem, smem, smem, smem],
-        out_specs=(vmem, vmem, vmem, vmem),
+        out_specs=(vmem, hbm, hbm),
         scratch_shapes=[
             pltpu.VMEM((nq, width, pw), bf16),
             pltpu.VMEM((nq, width, pw), bf16),
             pltpu.VMEM((nq, pw, width), bf16),
             pltpu.VMEM((nt, 2 * tr, width), bf16),
+            pltpu.VMEM((rows, width), bf16),
+            pltpu.VMEM((rows, width), bf16),
             pltpu.VMEM((nchunk, nchip) + piece, f32),
             pltpu.VMEM((nchunk, nchip) + piece, f32),
             pltpu.VMEM((nchunk, nchip) + piece, f32),
@@ -344,7 +377,7 @@
             pltpu.VMEM((rows, width), f32),
             pltpu.VMEM((nt, tr, width), f32),
             pltpu.VMEM((nt, tr, width), f32),
-            dma((nq, 3)),
+            dma((nq, 3)), dma((nchunk + 1,)),
             dma((nt,)), dma((nt,)),
             dma((nchunk, nchip)), dma((nchunk, nchip)),
             dma((nchunk, nchip)), dma((nchunk, nchip)),
@@ -358,32 +391,33 @@
         name="exchange",
     )(tokens, out_grad, gate_weight, up_weight, down_weight, gate_mask, up_mask, down_mask, counts)
 
-    whole = lambda q, *_: (0, 0)
-    gate_sum, up_sum, down_sum = pl.pallas_call(
+    d_tokens, gate_sum, up_sum, down_sum = pl.pallas_call(
         functools.partial(outer_kernel, pw),
         grid_spec=pltpu.PrefetchScalarGridSpec(
             num_scalar_prefetch=3,
             grid=(nq,),
             in_specs=[
-                pl.BlockSpec((rows, width), whole),
-                pl.BlockSpec((rows, width), whole),
+                pl.BlockSpec((nt, 2 * tr, width), lambda q, *_: (0, 0, 0)),
                 pl.BlockSpec((1,) + piece, lambda q, *_: (q, 0, 0, 0)),
+                pl.BlockSpec((tr, width), lambda q, *_: (0, 0)),
             ],
             out_specs=[
+                pl.BlockSpec((tr, width), lambda q, *_: (0, 0)),
                 pl.BlockSpec((width, pw), lambda q, *_: (0, q)),
                 pl.BlockSpec((width, pw), lambda q, *_: (0, q)),
                 pl.BlockSpec((pw, width), lambda q, *_: (q, 0)),
             ],
-            scratch_shapes=[pltpu.VMEM((width, rows), bf16)],
+            scratch_shapes=[pltpu.VMEM((width, rows), bf16), pltpu.VMEM((rows, width), bf16)],
         ),
         out_shape=(
+            jax.ShapeDtypeStruct((tr, width), bf16),
             jax.ShapeDtypeStruct((width, hidden_width), f32),
             jax.ShapeDtypeStruct((width, hidden_width), f32),
             jax.ShapeDtypeStruct((hidden_width, width), f32),
         ),
-        compiler_params=pltpu.CompilerParams(vmem_limit_bytes=40 * 2**20),
+        compiler_params=pltpu.CompilerParams(vmem_limit_bytes=60 * 2**20),
         name="outer",
-    )(gate_mask, up_mask, down_mask, tok_all, cot_all, act)
+    )(gate_mask, up_mask, down_mask, gathered, act, d_tokens)
     return d_tokens, gate_sum, up_sum, down_sum
 
 

time: 66.4 us -> 61.6 us (0.928)
  local copies, waits for them, and re-layouts: 5.52 us -> 0 us
  Pallas kernels: 59.1 us -> 60 us
    unnamed x14 -> x0, local copies, waits for them, and re-layouts: 5.52 us -> none
    pallas_call x1, Pallas kernels: 17.4 us -> 18.2 us  [on_device(): pl.pallas_call(functools.partial(outer_kernel, pw), grid_spec=pltpu.Prefe...]
where the time goes in v2:
time: 61.6 us; the launch traced here: 61.3 us
  Pallas kernels  60 us (97%)
  between operations  1.29 us (2%)
    pallas_call x1, Pallas kernels, on_device(): pl.pallas_call(functools.partial(exchange_kernel, ndp, nt, nq, pw, nchunk...  41.8 us
    pallas_call x1, Pallas kernels, on_device(): pl.pallas_call(functools.partial(outer_kernel, pw), grid_spec=pltpu.Prefe...  18.2 us

profile of v2, /device:TPU:0, one launch (start us, length us, event | category | flops | bytes accessed | tf_op | source)
XLA Modules:
  0.0 61.3 jit_solution(12938262243842499908)
XLA Ops:
  1.3 41.8 %exchange.1 = (bf16[8,1024]{1,0:T(8,128)(2,1)}, bf16[16,3,32,256]{3,2,1,0:T(8,128)(2,1)}, bf16[4,16,1024]{2,1,0:T(8,128)(2,1)}) custom-call(bf16[8,1024]{1,0:T(8,128)(2,1)} %tok_ref.1, bf16[8,1024]{1,0:T(8,128)(2,1)} %cot_ref.1, bf16[1024,3840]{1,0:T(8,128)(2,1)} %gate_hbm.1, bf16[1024,3840]{1,0:T(8,128)(2,1)} %up_hbm.1, bf16[3840,1024]{1,0:T(8,128)(2,1)} %down_hbm.1, ...), custom_call_target="tpu_custom_call" | custom-call | tf_op jit(solution)/shard_map/exchange/pallas_call | solution.py:355
  43.1 18.2 %outer.1 = (bf16[8,1024]{1,0:T(8,128)(2,1)}, f32[1024,3840]{1,0:T(8,128)}, f32[1024,3840]{1,0:T(8,128)}, f32[3840,1024]{1,0:T(8,128)}) custom-call(s32[8,30]{1,0:T(8,128)} %gmask.3, s32[8,30]{1,0:T(8,128)} %umask.3, s32[8,30]{1,0:T(8,128)} %bitcast.2, bf16[4,16,1024]{2,1,0:T(8,128)(2,1)} %get-tuple-element.7.x_ref, ...), custom_call_target="tpu_custom_call" | custom-call | tf_op jit(solution)/shard_map/outer/pallas_call | solution.py:394

commit v3 on v2

--- a/solution.py
+++ b/solution.py
@@ -9,6 +9,7 @@
 
 MESH = pl.DeviceIdType.MESH
 LANES = 128
+AHEAD = 6
 bf16, f32 = jnp.bfloat16, jnp.float32
 
 
@@ -71,17 +72,17 @@
     def each_piece(c, k, last):
         return c * ndp + 2 * k + (core if last else 1 - core)
 
-    for c in range(nchunk):
-        def load(k, _, c=c):
-            for last in (False, True):
-                q = each_piece(c, k, last)
-
-                @pl.when(q < nq)
-                def _():
-                    for copy in weight_copies(q):
-                        copy.start()
-            return 0
-        lax.fori_loop(0, nchip, load, 0)
+    def load(i, _):
+        within = lax.rem(i, ndp)
+        q = (i // ndp) * ndp + (within // 2) * 2 + jnp.where(lax.rem(i, 2) == 0, 1 - core, core)
+
+        @pl.when(jnp.logical_and(i < nchunk * ndp, q < nq))
+        def _():
+            for copy in weight_copies(q):
+                copy.start()
+        return 0
+
+    lax.fori_loop(0, AHEAD, load, 0)
 
     live = lax.broadcasted_iota(jnp.int32, (tr, width), 0) < counts[0]
     cot = jnp.where(live, cot_ref[...].astype(f32), 0.0)
@@ -156,13 +157,15 @@
             src_ref=snd1.at[c, k], dst_ref=rcv1.at[c, k], send_sem=s1_s.at[c, k],
             recv_sem=s1_r.at[c, k], device_id=(sibling, mt), device_id_type=MESH)
 
-    def forward(c):
+    def forward(c, lo, hi):
         def step(k, _):
+            load(c * ndp + 2 * k + AHEAD, 0)
             forward_piece(each_piece(c, k, False), snd1.at[c, k])
             copy1(c, k).start()
+            load(c * ndp + 2 * k + 1 + AHEAD, 0)
             forward_piece(each_piece(c, k, True), own1.at[c, k])
             return 0
-        lax.fori_loop(0, nchip, step, 0)
+        lax.fori_loop(lo, hi, step, 0)
 
     def copy2(c, slot, k):
         return pltpu.make_async_remote_copy(
@@ -247,9 +250,10 @@
 
     dacc[...] = jnp.zeros(dacc.shape, f32)
     for c in range(nchunk):
-        forward(c)
+        forward(c, 0, nchip // 2)
         if c > 0:
             activate(c - 1)
+        forward(c, nchip // 2, nchip)
         reduce_send(c)
         if c > 0:
             forward_on(c - 1)

time: 61.6 us -> 61.8 us (level)
  no operation moved by 1% of the time
where the time goes in v3:
time: 61.8 us; the launch traced here: 61.5 us
  Pallas kernels  60.2 us (97%)
  between operations  1.29 us (2%)
    pallas_call x1, Pallas kernels, on_device(): pl.pallas_call(functools.partial(exchange_kernel, ndp, nt, nq, pw, nchunk...  42 us
    pallas_call x1, Pallas kernels, on_device(): pl.pallas_call(functools.partial(outer_kernel, pw), grid_spec=pltpu.Prefe...  18.2 us

profile of v3, /device:TPU:0, one launch (start us, length us, event | category | flops | bytes accessed | tf_op | source)
XLA Modules:
  0.0 61.5 jit_solution(13607675635974114058)
XLA Ops:
  1.3 42.0 %exchange.1 = (bf16[8,1024]{1,0:T(8,128)(2,1)}, bf16[16,3,32,256]{3,2,1,0:T(8,128)(2,1)}, bf16[4,16,1024]{2,1,0:T(8,128)(2,1)}) custom-call(bf16[8,1024]{1,0:T(8,128)(2,1)} %tok_ref.1, bf16[8,1024]{1,0:T(8,128)(2,1)} %cot_ref.1, bf16[1024,3840]{1,0:T(8,128)(2,1)} %gate_hbm.1, bf16[1024,3840]{1,0:T(8,128)(2,1)} %up_hbm.1, bf16[3840,1024]{1,0:T(8,128)(2,1)} %down_hbm.1, ...), custom_call_target="tpu_custom_call" | custom-call | tf_op jit(solution)/shard_map/exchange/pallas_call | solution.py:359
  43.3 18.2 %outer.1 = (bf16[8,1024]{1,0:T(8,128)(2,1)}, f32[1024,3840]{1,0:T(8,128)}, f32[1024,3840]{1,0:T(8,128)}, f32[3840,1024]{1,0:T(8,128)}) custom-call(s32[8,30]{1,0:T(8,128)} %gmask.3, s32[8,30]{1,0:T(8,128)} %umask.3, s32[8,30]{1,0:T(8,128)} %bitcast.2, bf16[4,16,1024]{2,1,0:T(8,128)(2,1)} %get-tuple-element.7.x_ref, ...), custom_call_target="tpu_custom_call" | custom-call | tf_op jit(solution)/shard_map/outer/pallas_call | solution.py:398
